TPU v7x, 512 devices: a whole 4x8x8 slice. The times are simulated.
512 devices in a mesh: tm: 32 (over z, x), rows: 16 (over y, core).
Axes of the slice: x: 4, y: 8, z: 8, core: 2. Of those that a mesh axis runs over, the one named last changes fastest.
Arguments:
- frames: bfloat16 [64, 128, 48, 128], P('tm', 'rows'), may hold values from -60 to 60
- lengths: int32 [8], replicated, may hold values from 1 to 16, as said below
- norm_gain_one: float32 [128], replicated, may hold values from 0.5 to 1.5
- norm_shift_one: float32 [128], replicated, may hold values from -0.5 to 0.5
- conv_one: bfloat16 [3, 3, 3, 128, 128], replicated, may hold values from -0.109375 to 0.109375
- bias_one: float32 [128], replicated, may hold values from -1 to 1
- norm_gain_two: float32 [128], replicated, may hold values from 0.5 to 1.5
- norm_shift_two: float32 [128], replicated, may hold values from -0.5 to 0.5
- conv_two: bfloat16 [3, 3, 3, 128, 128], replicated, may hold values from -0.109375 to 0.109375
- bias_two: float32 [128], replicated, may hold values from -1 to 1
Outputs:
- encoded: float32 [64, 128, 48, 128], P('tm', 'rows')
Inputs may be any that keep to these rules, and one draw needn't show every extreme that they name: 8 video lengths that sum to 64; the longest has exactly 16 frames.
All inputs are finite; a program needn't handle non-finite values.
Results may differ from a plain program's by a relative error of at most 0.0014.
Values may be sent and summed in bfloat16 or wider, within the bound.
A program may use at most 64 MiB of HBM per device.

v0:
```python
import jax
import jax.numpy as jnp
from jax import lax
from jax.sharding import PartitionSpec as P

GROUPS = 32


def shifted(block, axis, distance):
    devices = range(lax.axis_size(axis))
    route = [(i - distance, i) for i in devices if i - distance in devices]
    return lax.ppermute(block, axis, route)


def extended(cells, sides, width):
    for axis, dim in sides:
        count = lax.axis_size(axis)
        ends = count - 1
        head = lax.slice_in_dim(cells, 0, width, axis=dim)
        tail = lax.slice_in_dim(cells, cells.shape[dim] - width, cells.shape[dim], axis=dim)
        cells = jnp.concatenate(
            [
                lax.ppermute(tail, axis, [(i, (i + 1) % count) for i in range(ends)]),
                cells,
                lax.ppermute(head, axis, [((i + 1) % count, i) for i in range(ends)]),
            ],
            axis=dim,
        )
    return cells


def plan_frames(lengths, count, first):
    videos = lengths.shape[0]
    offsets = jnp.cumsum(lengths) - lengths
    frame_ids = first + jnp.arange(count, dtype=jnp.int32)
    inside = offsets[None, :] <= frame_ids[:, None]
    video = jnp.sum(inside.astype(jnp.int32), axis=1) - 1
    starts = jnp.max(jnp.where(inside, offsets[None, :], 0), axis=1)
    onehot = (video[:, None] == jnp.arange(videos, dtype=jnp.int32)[None, :]).astype(jnp.float32)
    taps = [jnp.maximum(frame_ids - back, starts) - first + 2 for back in (2, 1, 0)]
    return (onehot, taps)


def group_totals(values):
    count = values.shape[0]
    width = values.shape[3]
    return jnp.sum(values, axis=(1, 2)).reshape(count, GROUPS, width // GROUPS).sum(-1)


def spread_groups(table, onehot, width):
    return jnp.repeat(
        jnp.dot(onehot, table, precision=lax.Precision.HIGHEST), width // GROUPS, axis=1
    )


def group_norm(values, onehot, counts, gain, shift):
    width = values.shape[3]
    sums = jnp.dot(onehot.T, group_totals(values), precision=lax.Precision.HIGHEST)
    mean = lax.psum(sums, ("tm", "rows")) / counts[:, None]
    centered = values - spread_groups(mean, onehot, width)[:, None, None, :]
    squares = jnp.dot(onehot.T, group_totals(centered * centered), precision=lax.Precision.HIGHEST)
    var = lax.psum(squares, ("tm", "rows")) / counts[:, None]
    scale = spread_groups(lax.rsqrt(var + 1e-06), onehot, width)
    return centered * scale[:, None, None, :] * gain + shift


def causal_conv(act, weight, bias, taps):
    count, height, cols_n, width = act.shape
    prior = shifted(act, "tm", 1)
    joined = jnp.concatenate([prior, act], axis=0)
    rimmed = extended(joined, (("rows", 1),), 1)
    padded = jnp.pad(rimmed, ((0, 0), (0, 0), (1, 1), (0, 0)))
    columns = jnp.concatenate(
        [padded[:, :, shift_col : shift_col + cols_n] for shift_col in range(3)], axis=-1
    )
    total = jnp.zeros((count * height * cols_n, width), jnp.float32)
    for step in range(3):
        picked = jnp.take(columns, taps[step], axis=0)
        for row_off in range(3):
            slab = picked[:, row_off : row_off + height].reshape(count * height * cols_n, 3 * width)
            kernel = weight[step, row_off].reshape(3 * width, width)
            total = total + jnp.dot(slab, kernel, preferred_element_type=jnp.float32)
    return total.reshape(count, height, cols_n, width) + bias


def per_device(
    frames,
    lengths,
    norm_gain_one,
    norm_shift_one,
    conv_one,
    bias_one,
    norm_gain_two,
    norm_shift_two,
    conv_two,
    bias_two,
):
    count, height, cols_n, width = frames.shape
    first = lax.axis_index("tm") * count
    onehot, taps = plan_frames(lengths, count, first)
    full_height = height * lax.axis_size("rows")
    counts = lengths.astype(jnp.float32) * (full_height * cols_n * (width // GROUPS))
    values = frames.astype(jnp.float32)
    act_one = jax.nn.silu(group_norm(values, onehot, counts, norm_gain_one, norm_shift_one)).astype(
        jnp.bfloat16
    )
    middle = causal_conv(act_one, conv_one, bias_one, taps).astype(jnp.bfloat16)
    act_two = jax.nn.silu(
        group_norm(middle.astype(jnp.float32), onehot, counts, norm_gain_two, norm_shift_two)
    ).astype(jnp.bfloat16)
    return values + causal_conv(act_two, conv_two, bias_two, taps)


def solution(mesh):
    placed = (P("tm", "rows", None, None), P(), P(), P(), P(), P(), P(), P(), P(), P())
    return jax.shard_map(
        per_device,
        mesh=mesh,
        in_specs=placed,
        out_specs=P("tm", "rows", None, None),
        check_vma=False,
    )
```

profile of v0, /device:TPU:89, one launch (start us, length us, event | category | flops | bytes accessed | tf_op | source)
XLA Modules:
  0.0 459.6 jit_solution(9391679192439192227)
XLA Ops:
  0.0 0.7 convert_multiply_fusion
  0.7 0.8 reduce-window.9
  1.6 0.7 bitcast_subtract_fusion
  2.4 1.0 convert_reduce_fusion
  3.6 0.3 fusion.56
  3.9 101.7 %psum.28 = f32[8,32]{1,0:T(8,128)S(1)} all-reduce(f32[8,32]{1,0:T(8,128)S(1)} %fusion.56), channel_id=1, replica_groups=mesh['tm'=32,'rows'=16] {'tm','rows'}, use_global_device_ids=true, to_apply=%region_4.5 | all-reduce | flops 256 | bytes 2048 | tf_op jit(solution)/shard_map/psum | solution.py:59
  106.0 1.0 fusion.15
  107.2 0.3 fusion.55
  107.5 94.3 %psum.29 = f32[8,32]{1,0:T(8,128)S(1)} all-reduce(f32[8,32]{1,0:T(8,128)S(1)} %fusion.55), channel_id=1, replica_groups=mesh['tm'=32,'rows'=16] {'tm','rows'}, use_global_device_ids=true, to_apply=%region_7.8 | all-reduce | flops 256 | bytes 2048 | tf_op jit(solution)/shard_map/psum | solution.py:62
  202.2 1.1 fusion.23
  203.3 3.7 collective-permute-start
  207.1 1.0 fusion.68
  208.1 5.6 %collective-permute-done = bf16[2,8,48,128]{3,2,1,0:T(8,128)(2,1)S(1)} collective-permute-done((bf16[2,8,48,128]{3,2,1,0:T(8,128)(2,1)S(1)}, bf16[2,8,48,128]{3,2,1,0:T(8,128)(2,1)S(1)}, u32[]{:S(2)}, u32[]{:S(2)}) %collective-permute-start) | collective-permute-done | bytes 196640 | tf_op jit(solution)/shard_map/ppermute | solution.py:12
  213.7 5.1 %collective-permute-start.1 = (bf16[4,1,48,128]{3,2,1,0:T(8,128)(2,1)S(1)}, bf16[4,1,48,128]{3,2,1,0:T(8,128)(2,1)S(1)}, u32[]{:S(2)}, u32[]{:S(2)}) collective-permute-start(bf16[4,1,48,128]{3,2,1,0:T(8,128)(2,1)S(1)} %get-tuple-element.58), channel_id=1, source_target_pairs={{0,1},{1,2},{2,3},{3,4},{4,5},{5,6},{6,7},{7,8},{8,9},{9,10},{10,1... | collective-permute-start | bytes 147464 | tf_op jit(solution)/shard_map/ppermute | solution.py:23
  218.8 1.9 collective-permute-start.2
  220.8 4.7 %collective-permute-done.2 = bf16[4,1,48,128]{3,2,1,0:T(8,128)(2,1)S(1)} collective-permute-done((bf16[4,1,48,128]{3,2,1,0:T(8,128)(2,1)S(1)}, bf16[4,1,48,128]{3,2,1,0:T(8,128)(2,1)S(1)}, u32[]{:S(2)}, u32[]{:S(2)}) %collective-permute-start.2) | collective-permute-done | bytes 49184 | tf_op jit(solution)/shard_map/ppermute | solution.py:25
  225.5 0.2 fusion.8
  225.7 0.3 fusion.76
  226.2 0.7 gather_fusion.2
  226.9 1.5 gather_fusion
  228.4 1.3 broadcast_select_fusion
  229.8 1.2 fusion.74
  231.0 0.7 gather_fusion.1
  232.2 0.7 copy-done.13
  232.9 0.3 fusion.77
  233.3 0.3 convolution_add_fusion.15
  233.6 0.3 convolution_add_fusion.14
  233.9 0.3 copy-done.10
  234.2 0.3 convolution_add_fusion.13
  234.5 0.3 convolution_add_fusion.12
  235.1 0.3 convolution_add_fusion.11
  235.4 0.3 convolution_add_fusion.10
  235.8 0.2 copy-done.6
  236.0 0.3 convolution_add_fusion.9
  236.4 0.3 convolution_add_fusion.8
  237.0 0.3 fusion.54
  237.2 94.4 %psum.30 = f32[8,32]{1,0:T(8,128)S(1)} all-reduce(f32[8,32]{1,0:T(8,128)S(1)} %fusion.54), channel_id=1, replica_groups=mesh['tm'=32,'rows'=16] {'tm','rows'}, use_global_device_ids=true, to_apply=%region_11.13 | all-reduce | flops 256 | bytes 2048 | tf_op jit(solution)/shard_map/psum | solution.py:59
  332.3 0.3 fusion.53
  332.6 94.1 %psum.31 = f32[8,32]{1,0:T(8,128)S(1)} all-reduce(f32[8,32]{1,0:T(8,128)S(1)} %fusion.53), channel_id=1, replica_groups=mesh['tm'=32,'rows'=16] {'tm','rows'}, use_global_device_ids=true, to_apply=%region_14.16 | all-reduce | flops 256 | bytes 2048 | tf_op jit(solution)/shard_map/psum | solution.py:62
  427.2 2.8 collective-permute-start.3
  430.0 7.0 %collective-permute-done.3 = bf16[2,8,48,128]{3,2,1,0:T(8,128)(2,1)S(1)} collective-permute-done((bf16[2,8,48,128]{3,2,1,0:T(8,128)(2,1)S(1)}, bf16[2,8,48,128]{3,2,1,0:T(8,128)(2,1)S(1)}, u32[]{:S(2)}, u32[]{:S(2)}) %collective-permute-start.3) | collective-permute-done | bytes 196640 | tf_op jit(solution)/shard_map/ppermute | solution.py:12
  437.0 5.1 %collective-permute-start.4 = (bf16[4,1,48,128]{3,2,1,0:T(8,128)(2,1)S(1)}, bf16[4,1,48,128]{3,2,1,0:T(8,128)(2,1)S(1)}, u32[]{:S(2)}, u32[]{:S(2)}) collective-permute-start(bf16[4,1,48,128]{3,2,1,0:T(8,128)(2,1)S(1)} %get-tuple-element.56), channel_id=1, source_target_pairs={{0,1},{1,2},{2,3},{3,4},{4,5},{5,6},{6,7},{7,8},{8,9},{9,10},{10,1... | collective-permute-start | bytes 147464 | tf_op jit(solution)/shard_map/ppermute | solution.py:23
  442.1 2.1 collective-permute-start.5
  444.2 0.8 fusion.67
  444.9 3.7 collective-permute-done.5
  448.7 0.2 select_maximum_fusion
  448.9 0.3 fusion.75
  449.4 1.5 gather_fusion.3
  450.9 0.7 gather_fusion.4
  451.6 0.7 gather_fusion.5
  452.4 1.3 broadcast_select_fusion.1
  454.1 0.4 copy-done.18
  454.9 0.7 copy-done.16
  455.6 0.3 fusion.78
  455.9 0.3 convolution_add_fusion.7
  456.3 0.3 convolution_add_fusion.6
  456.6 0.3 convolution_add_fusion.5
  456.9 0.3 convolution_add_fusion.4
  457.3 0.3 convolution_add_fusion.3
  457.6 0.3 convolution_add_fusion.2
  457.9 0.3 convolution_add_fusion.1
  458.3 0.3 convolution_add_fusion
  458.6 0.3 copy-done
  458.8 0.8 convert_add_fusion
  (96 shorter events, 4.9 us)
Async XLA Ops:
  0.0 207.1 %copy-start.3 = (bf16[3,3,3,128,128]{4,3,2,1,0:T(8,128)(2,1)S(1)}, bf16[3,3,3,128,128]{4,3,2,1,0:T(8,128)(2,1)}, u32[]{:S(2)}) copy-start(bf16[3,3,3,128,128]{4,3,2,1,0:T(8,128)(2,1)} %param.16) | copy-start | bytes 2654212
  0.7 207.3 %copy-start.25 = (f32[8]{0:T(128)}, f32[8]{0:T(128)S(1)}, u32[]{:S(2)}) copy-start(f32[8]{0:T(128)S(1)} %convert_multiply_fusion) | copy-start | bytes 100
  2.4 205.6 %copy-start.27 = (s32[2]{0:T(128)}, s32[2]{0:T(128)S(1)}, u32[]{:S(2)}) copy-start(s32[2]{0:T(128)S(1)} %broadcast_add_fusion) | copy-start | bytes 28
  203.3 10.4 %collective-permute-start = (bf16[2,8,48,128]{3,2,1,0:T(8,128)(2,1)S(1)}, bf16[2,8,48,128]{3,2,1,0:T(8,128)(2,1)S(1)}, u32[]{:S(2)}, u32[]{:S(2)}) collective-permute-start(bf16[2,8,48,128]{3,2,1,0:T(8,128)(2,1)S(1)} %fusion.23), channel_id=1, source_target_pairs={{0,16},{16,32},{32,48},{48,64},{64,80},{80,96},{96,112},{112,128},... | collective-permute-start | bytes 589832 | tf_op jit(solution)/shard_map/ppermute | solution.py:12
  207.0 21.4 %copy-start.17 = (pred[2]{0:T(512)(128)(4,1)}, pred[2]{0:T(512)(128)(4,1)S(1)}, u32[]{:S(2)}) copy-start(pred[2]{0:T(512)(128)(4,1)S(1)} %get-tuple-element.10) | copy-start | bytes 10
  207.0 21.4 %copy-start.19 = (pred[2]{0:T(512)(128)(4,1)}, pred[2]{0:T(512)(128)(4,1)S(1)}, u32[]{:S(2)}) copy-start(pred[2]{0:T(512)(128)(4,1)S(1)} %get-tuple-element.62) | copy-start | bytes 10
  213.7 7.1 %collective-permute-start.1 = (bf16[4,1,48,128]{3,2,1,0:T(8,128)(2,1)S(1)}, bf16[4,1,48,128]{3,2,1,0:T(8,128)(2,1)S(1)}, u32[]{:S(2)}, u32[]{:S(2)}) collective-permute-start(bf16[4,1,48,128]{3,2,1,0:T(8,128)(2,1)S(1)} %get-tuple-element.58), channel_id=1, source_target_pairs={{0,1},{1,2},{2,3},{3,4},{4,5},{5,6},{6,7},{7,8},{8,9},{9,10},{10,1... | collective-permute-start | bytes 147464 | tf_op jit(solution)/shard_map/ppermute | solution.py:23
  218.8 6.6 %collective-permute-start.2 = (bf16[4,1,48,128]{3,2,1,0:T(8,128)(2,1)S(1)}, bf16[4,1,48,128]{3,2,1,0:T(8,128)(2,1)S(1)}, u32[]{:S(2)}, u32[]{:S(2)}) collective-permute-start(bf16[4,1,48,128]{3,2,1,0:T(8,128)(2,1)S(1)} %get-tuple-element.59), channel_id=1, source_target_pairs={{1,0},{2,1},{3,2},{4,3},{5,4},{6,5},{7,6},{8,7},{9,8},{10,9},{11,1... | collective-permute-start | bytes 147464 | tf_op jit(solution)/shard_map/ppermute | solution.py:25
  232.0 0.9 copy-start.13
  232.0 1.2 copy-start.2
  232.0 1.2 copy-start.12
  232.2 1.4 copy-start.1
  232.2 1.4 copy-start.11
  233.3 0.9 copy-start.10
  233.6 0.9 copy-start.9
  234.2 0.9 copy-start.8
  234.5 0.9 copy-start.7
  235.1 0.9 copy-start.6
  235.4 0.9 copy-start.5
  236.0 0.7 copy-start.24
  236.0 1.0 copy-start.28
  236.3 95.3 %copy-start.26 = (f32[8]{0:T(128)S(1)}, f32[8]{0:T(128)}, u32[]{:S(2)}) copy-start(f32[8]{0:T(128)} %copy-done.25) | copy-start | bytes 100
  236.3 190.7 %copy-start.22 = (f32[128]{0:T(128)S(1)}, f32[128]{0:T(128)}, u32[]{:S(2)}) copy-start(f32[128]{0:T(128)} %param.19) | copy-start | bytes 1540
  236.3 190.7 %copy-start.23 = (f32[128]{0:T(128)S(1)}, f32[128]{0:T(128)}, u32[]{:S(2)}) copy-start(f32[128]{0:T(128)} %param.18) | copy-start | bytes 1540
  236.7 207.5 %copy-start.4 = (bf16[3,3,3,128,128]{4,3,2,1,0:T(8,128)(2,1)S(1)}, bf16[3,3,3,128,128]{4,3,2,1,0:T(8,128)(2,1)}, u32[]{:S(2)}) copy-start(bf16[3,3,3,128,128]{4,3,2,1,0:T(8,128)(2,1)} %param.20) | copy-start | bytes 2654212
  427.2 9.8 %collective-permute-start.3 = (bf16[2,8,48,128]{3,2,1,0:T(8,128)(2,1)S(1)}, bf16[2,8,48,128]{3,2,1,0:T(8,128)(2,1)S(1)}, u32[]{:S(2)}, u32[]{:S(2)}) collective-permute-start(bf16[2,8,48,128]{3,2,1,0:T(8,128)(2,1)S(1)} %fusion.32), channel_id=1, source_target_pairs={{0,16},{16,32},{32,48},{48,64},{64,80},{80,96},{96,112},{112,128},... | collective-permute-start | bytes 589832 | tf_op jit(solution)/shard_map/ppermute | solution.py:12
  437.0 8.0 %collective-permute-start.4 = (bf16[4,1,48,128]{3,2,1,0:T(8,128)(2,1)S(1)}, bf16[4,1,48,128]{3,2,1,0:T(8,128)(2,1)S(1)}, u32[]{:S(2)}, u32[]{:S(2)}) collective-permute-start(bf16[4,1,48,128]{3,2,1,0:T(8,128)(2,1)S(1)} %get-tuple-element.56), channel_id=1, source_target_pairs={{0,1},{1,2},{2,3},{3,4},{4,5},{5,6},{6,7},{7,8},{8,9},{9,10},{10,1... | collective-permute-start | bytes 147464 | tf_op jit(solution)/shard_map/ppermute | solution.py:23
  442.1 6.6 %collective-permute-start.5 = (bf16[4,1,48,128]{3,2,1,0:T(8,128)(2,1)S(1)}, bf16[4,1,48,128]{3,2,1,0:T(8,128)(2,1)S(1)}, u32[]{:S(2)}, u32[]{:S(2)}) collective-permute-start(bf16[4,1,48,128]{3,2,1,0:T(8,128)(2,1)S(1)} %get-tuple-element.57), channel_id=1, source_target_pairs={{1,0},{2,1},{3,2},{4,3},{5,4},{6,5},{7,6},{8,7},{9,8},{10,9},{11,1... | collective-permute-start | bytes 147464 | tf_op jit(solution)/shard_map/ppermute | solution.py:25
  450.9 1.4 copy-start.20
  454.0 0.6 copy-start.18
  454.7 0.9 copy-start.16
  454.7 1.2 copy-start.15
  454.9 1.4 copy-start.14
  457.9 0.9 copy-start
  457.9 0.9 copy-start.21
where the time goes:
time: 460 us
  blocking collectives  385 us (84%)
  waiting for transfers between devices  21 us (5%)
  starting transfers between devices  20.7 us (4%)
  local copies, waits for them, and re-layouts  14.3 us (3%)
  other arithmetic  11 us (2%)
  matrix products  7.45 us (2%)
    psum x2, blocking collectives, group_norm(): mean = lax.psum(sums, ('tm', 'rows')) / counts[:, None]  196 us
    psum x2, blocking collectives, group_norm(): var = lax.psum(squares, ('tm', 'rows')) / counts[:, None]  188 us
    ppermute x2, waiting for transfers between devices, shifted(): return lax.ppermute(block, axis, route)  12.6 us
    ppermute x2, starting transfers between devices, extended(): lax.ppermute(tail, axis, [(i, (i + 1) % count) for i in range(ends)])  10.2 us
  transfers between devices with their start and end apart: 6, of which 4 were waited for; matrix products, arithmetic and copies ran while one was open for 0% of the time, Pallas kernels for 0%

commit v1 on v0

--- a/solution.py
+++ b/solution.py
@@ -56,7 +56,7 @@
 def group_norm(values, onehot, counts, gain, shift):
     width = values.shape[3]
     sums = jnp.dot(onehot.T, group_totals(values), precision=lax.Precision.HIGHEST)
-    mean = lax.psum(sums, ("tm", "rows")) / counts[:, None]
+    mean = lax.psum(lax.psum(sums, "tm"), "rows") / counts[:, None]
     centered = values - spread_groups(mean, onehot, width)[:, None, None, :]
     squares = jnp.dot(onehot.T, group_totals(centered * centered), precision=lax.Precision.HIGHEST)
     var = lax.psum(squares, ("tm", "rows")) / counts[:, None]

time: 460 us -> 458 us (level)
  the two profiles are of different devices: /device:TPU:89 before, /device:TPU:27 now
where the time goes in v1:
time: 458 us; the launch traced here: 457 us
  blocking collectives  387 us (84%)
  waiting for transfers between devices  18.8 us (4%)
  starting transfers between devices  17.5 us (4%)
  local copies, waits for them, and re-layouts  14.3 us (3%)
  other arithmetic  11 us (2%)
  matrix products  7.45 us (2%)
    psum x2, blocking collectives, group_norm(): var = lax.psum(squares, ('tm', 'rows')) / counts[:, None]  198 us
    psum x4, blocking collectives, group_norm(): mean = lax.psum(lax.psum(sums, 'tm'), 'rows') / counts[:, None]  189 us
    ppermute x2, waiting for transfers between devices, shifted(): return lax.ppermute(block, axis, route)  10.4 us
    ppermute x2, starting transfers between devices, extended(): lax.ppermute(tail, axis, [(i, (i + 1) % count) for i in range(ends)])  9.65 us
  transfers between devices with their start and end apart: 6, of which 4 were waited for; matrix products, arithmetic and copies ran while one was open for 0% of the time, Pallas kernels for 0%

profile of v1, /device:TPU:27, one launch (start us, length us, event | category | flops | bytes accessed | tf_op | source)
XLA Modules:
  0.0 456.9 jit_solution(12541542253429955449)
XLA Ops:
  0.0 0.7 convert_multiply_fusion
  0.7 0.8 reduce-window.9
  1.6 0.7 bitcast_subtract_fusion
  2.4 1.0 convert_reduce_fusion
  3.6 0.3 fusion.56
  3.9 62.9 %psum.42 = f32[8,32]{1,0:T(8,128)S(1)} all-reduce(f32[8,32]{1,0:T(8,128)S(1)} %fusion.56), channel_id=1, replica_groups=mesh['tm'=32,'rows'=16] {'tm'}, use_global_device_ids=true, to_apply=%region_4.5 | all-reduce | flops 256 | bytes 2048 | tf_op jit(solution)/shard_map/psum | solution.py:59
  66.8 37.1 %psum.43 = f32[8,32]{1,0:T(8,128)S(1)} all-reduce(f32[8,32]{1,0:T(8,128)S(1)} %psum.42), channel_id=1, replica_groups=mesh['tm'=32,'rows'=16] {'rows'}, use_global_device_ids=true, to_apply=%region_5.6 | all-reduce | flops 256 | bytes 2048 | tf_op jit(solution)/shard_map/psum | solution.py:59
  104.3 1.0 fusion.15
  105.5 0.3 fusion.55
  105.7 99.5 %psum.44 = f32[8,32]{1,0:T(8,128)S(1)} all-reduce(f32[8,32]{1,0:T(8,128)S(1)} %fusion.55), channel_id=1, replica_groups=mesh['tm'=32,'rows'=16] {'tm','rows'}, use_global_device_ids=true, to_apply=%region_8.9 | all-reduce | flops 256 | bytes 2048 | tf_op jit(solution)/shard_map/psum | solution.py:62
  205.7 1.1 fusion.23
  206.8 1.9 collective-permute-start
  208.8 1.0 fusion.68
  209.7 4.7 %collective-permute-done = bf16[2,8,48,128]{3,2,1,0:T(8,128)(2,1)S(1)} collective-permute-done((bf16[2,8,48,128]{3,2,1,0:T(8,128)(2,1)S(1)}, bf16[2,8,48,128]{3,2,1,0:T(8,128)(2,1)S(1)}, u32[]{:S(2)}, u32[]{:S(2)}) %collective-permute-start) | collective-permute-done | bytes 196640 | tf_op jit(solution)/shard_map/ppermute | solution.py:12
  214.4 4.8 %collective-permute-start.1 = (bf16[4,1,48,128]{3,2,1,0:T(8,128)(2,1)S(1)}, bf16[4,1,48,128]{3,2,1,0:T(8,128)(2,1)S(1)}, u32[]{:S(2)}, u32[]{:S(2)}) collective-permute-start(bf16[4,1,48,128]{3,2,1,0:T(8,128)(2,1)S(1)} %get-tuple-element.58), channel_id=1, source_target_pairs={{0,1},{1,2},{2,3},{3,4},{4,5},{5,6},{6,7},{7,8},{8,9},{9,10},{10,1... | collective-permute-start | bytes 147464 | tf_op jit(solution)/shard_map/ppermute | solution.py:23
  219.3 1.9 collective-permute-start.2
  221.2 4.7 %collective-permute-done.2 = bf16[4,1,48,128]{3,2,1,0:T(8,128)(2,1)S(1)} collective-permute-done((bf16[4,1,48,128]{3,2,1,0:T(8,128)(2,1)S(1)}, bf16[4,1,48,128]{3,2,1,0:T(8,128)(2,1)S(1)}, u32[]{:S(2)}, u32[]{:S(2)}) %collective-permute-start.2) | collective-permute-done | bytes 49184 | tf_op jit(solution)/shard_map/ppermute | solution.py:25
  226.1 0.3 fusion.76
  226.6 0.7 gather_fusion.2
  227.3 1.5 gather_fusion
  228.9 1.3 broadcast_select_fusion
  230.2 1.2 fusion.74
  231.4 0.7 gather_fusion.1
  232.6 0.7 copy-done.13
  233.3 0.3 fusion.77
  233.7 0.3 convolution_add_fusion.15
  234.0 0.3 convolution_add_fusion.14
  234.3 0.3 copy-done.10
  234.6 0.3 convolution_add_fusion.13
  234.9 0.3 convolution_add_fusion.12
  235.5 0.3 convolution_add_fusion.11
  235.8 0.3 convolution_add_fusion.10
  236.2 0.2 copy-done.6
  236.4 0.3 convolution_add_fusion.9
  236.8 0.3 convolution_add_fusion.8
  237.4 0.3 fusion.54
  237.6 55.1 %psum.45 = f32[8,32]{1,0:T(8,128)S(1)} all-reduce(f32[8,32]{1,0:T(8,128)S(1)} %fusion.54), channel_id=1, replica_groups=mesh['tm'=32,'rows'=16] {'tm'}, use_global_device_ids=true, to_apply=%region_12.14 | all-reduce | flops 256 | bytes 2048 | tf_op jit(solution)/shard_map/psum | solution.py:59
  292.7 34.2 %psum.46 = f32[8,32]{1,0:T(8,128)S(1)} all-reduce(f32[8,32]{1,0:T(8,128)S(1)} %psum.45), channel_id=1, replica_groups=mesh['tm'=32,'rows'=16] {'rows'}, use_global_device_ids=true, to_apply=%region_13.15 | all-reduce | flops 256 | bytes 2048 | tf_op jit(solution)/shard_map/psum | solution.py:59
  327.6 0.3 fusion.53
  327.8 98.4 %psum.47 = f32[8,32]{1,0:T(8,128)S(1)} all-reduce(f32[8,32]{1,0:T(8,128)S(1)} %fusion.53), channel_id=1, replica_groups=mesh['tm'=32,'rows'=16] {'tm','rows'}, use_global_device_ids=true, to_apply=%region_16.18 | all-reduce | flops 256 | bytes 2048 | tf_op jit(solution)/shard_map/psum | solution.py:62
  426.8 1.9 collective-permute-start.3
  428.7 5.7 %collective-permute-done.3 = bf16[2,8,48,128]{3,2,1,0:T(8,128)(2,1)S(1)} collective-permute-done((bf16[2,8,48,128]{3,2,1,0:T(8,128)(2,1)S(1)}, bf16[2,8,48,128]{3,2,1,0:T(8,128)(2,1)S(1)}, u32[]{:S(2)}, u32[]{:S(2)}) %collective-permute-start.3) | collective-permute-done | bytes 196640 | tf_op jit(solution)/shard_map/ppermute | solution.py:12
  434.4 4.8 %collective-permute-start.4 = (bf16[4,1,48,128]{3,2,1,0:T(8,128)(2,1)S(1)}, bf16[4,1,48,128]{3,2,1,0:T(8,128)(2,1)S(1)}, u32[]{:S(2)}, u32[]{:S(2)}) collective-permute-start(bf16[4,1,48,128]{3,2,1,0:T(8,128)(2,1)S(1)} %get-tuple-element.56), channel_id=1, source_target_pairs={{0,1},{1,2},{2,3},{3,4},{4,5},{5,6},{6,7},{7,8},{8,9},{9,10},{10,1... | collective-permute-start | bytes 147464 | tf_op jit(solution)/shard_map/ppermute | solution.py:23
  439.3 2.1 collective-permute-start.5
  441.4 0.7 fusion.67
  442.2 3.7 collective-permute-done.5
  446.1 0.3 fusion.75
  446.6 1.5 gather_fusion.3
  448.2 0.7 gather_fusion.4
  448.9 0.7 gather_fusion.5
  449.6 1.3 broadcast_select_fusion.1
  451.4 0.5 copy-done.18
  452.2 0.7 copy-done.16
  452.9 0.3 fusion.78
  453.2 0.3 convolution_add_fusion.7
  453.6 0.3 convolution_add_fusion.6
  453.9 0.3 convolution_add_fusion.5
  454.2 0.3 convolution_add_fusion.4
  454.5 0.3 convolution_add_fusion.3
  454.9 0.3 convolution_add_fusion.2
  455.2 0.3 convolution_add_fusion.1
  455.5 0.3 convolution_add_fusion
  455.9 0.3 copy-done
  456.1 0.8 convert_add_fusion
  (98 shorter events, 5.3 us)
Async XLA Ops:
  0.0 208.8 %copy-start.3 = (bf16[3,3,3,128,128]{4,3,2,1,0:T(8,128)(2,1)S(1)}, bf16[3,3,3,128,128]{4,3,2,1,0:T(8,128)(2,1)}, u32[]{:S(2)}) copy-start(bf16[3,3,3,128,128]{4,3,2,1,0:T(8,128)(2,1)} %param.16) | copy-start | bytes 2654212
  0.7 209.0 %copy-start.25 = (f32[8]{0:T(128)}, f32[8]{0:T(128)S(1)}, u32[]{:S(2)}) copy-start(f32[8]{0:T(128)S(1)} %convert_multiply_fusion) | copy-start | bytes 100
  2.4 207.3 %copy-start.27 = (s32[2]{0:T(128)}, s32[2]{0:T(128)S(1)}, u32[]{:S(2)}) copy-start(s32[2]{0:T(128)S(1)} %broadcast_add_fusion) | copy-start | bytes 28
  206.8 7.7 %collective-permute-start = (bf16[2,8,48,128]{3,2,1,0:T(8,128)(2,1)S(1)}, bf16[2,8,48,128]{3,2,1,0:T(8,128)(2,1)S(1)}, u32[]{:S(2)}, u32[]{:S(2)}) collective-permute-start(bf16[2,8,48,128]{3,2,1,0:T(8,128)(2,1)S(1)} %fusion.23), channel_id=1, source_target_pairs={{0,16},{16,32},{32,48},{48,64},{64,80},{80,96},{96,112},{112,128},... | collective-permute-start | bytes 589832 | tf_op jit(solution)/shard_map/ppermute | solution.py:12
  208.7 20.1 %copy-start.17 = (pred[2]{0:T(512)(128)(4,1)}, pred[2]{0:T(512)(128)(4,1)S(1)}, u32[]{:S(2)}) copy-start(pred[2]{0:T(512)(128)(4,1)S(1)} %get-tuple-element.10) | copy-start | bytes 10
  208.7 20.1 %copy-start.19 = (pred[2]{0:T(512)(128)(4,1)}, pred[2]{0:T(512)(128)(4,1)S(1)}, u32[]{:S(2)}) copy-start(pred[2]{0:T(512)(128)(4,1)S(1)} %get-tuple-element.62) | copy-start | bytes 10
  214.4 6.8 %collective-permute-start.1 = (bf16[4,1,48,128]{3,2,1,0:T(8,128)(2,1)S(1)}, bf16[4,1,48,128]{3,2,1,0:T(8,128)(2,1)S(1)}, u32[]{:S(2)}, u32[]{:S(2)}) collective-permute-start(bf16[4,1,48,128]{3,2,1,0:T(8,128)(2,1)S(1)} %get-tuple-element.58), channel_id=1, source_target_pairs={{0,1},{1,2},{2,3},{3,4},{4,5},{5,6},{6,7},{7,8},{8,9},{9,10},{10,1... | collective-permute-start | bytes 147464 | tf_op jit(solution)/shard_map/ppermute | solution.py:23
  219.3 6.6 %collective-permute-start.2 = (bf16[4,1,48,128]{3,2,1,0:T(8,128)(2,1)S(1)}, bf16[4,1,48,128]{3,2,1,0:T(8,128)(2,1)S(1)}, u32[]{:S(2)}, u32[]{:S(2)}) collective-permute-start(bf16[4,1,48,128]{3,2,1,0:T(8,128)(2,1)S(1)} %get-tuple-element.59), channel_id=1, source_target_pairs={{1,0},{2,1},{3,2},{4,3},{5,4},{6,5},{7,6},{8,7},{9,8},{10,9},{11,1... | collective-permute-start | bytes 147464 | tf_op jit(solution)/shard_map/ppermute | solution.py:25
  232.4 0.9 copy-start.13
  232.4 1.2 copy-start.2
  232.4 1.2 copy-start.12
  232.6 1.4 copy-start.1
  232.6 1.4 copy-start.11
  233.7 0.9 copy-start.10
  234.0 0.9 copy-start.9
  234.6 0.9 copy-start.8
  234.9 0.9 copy-start.7
  235.5 0.9 copy-start.6
  235.8 0.9 copy-start.5
  236.4 0.7 copy-start.24
  236.4 1.0 copy-start.28
  236.7 90.2 %copy-start.26 = (f32[8]{0:T(128)S(1)}, f32[8]{0:T(128)}, u32[]{:S(2)}) copy-start(f32[8]{0:T(128)} %copy-done.25) | copy-start | bytes 100
  236.7 189.9 %copy-start.22 = (f32[128]{0:T(128)S(1)}, f32[128]{0:T(128)}, u32[]{:S(2)}) copy-start(f32[128]{0:T(128)} %param.19) | copy-start | bytes 1540
  236.7 189.9 %copy-start.23 = (f32[128]{0:T(128)S(1)}, f32[128]{0:T(128)}, u32[]{:S(2)}) copy-start(f32[128]{0:T(128)} %param.18) | copy-start | bytes 1540
  237.1 204.3 %copy-start.4 = (bf16[3,3,3,128,128]{4,3,2,1,0:T(8,128)(2,1)S(1)}, bf16[3,3,3,128,128]{4,3,2,1,0:T(8,128)(2,1)}, u32[]{:S(2)}) copy-start(bf16[3,3,3,128,128]{4,3,2,1,0:T(8,128)(2,1)} %param.20) | copy-start | bytes 2654212
  426.8 7.7 %collective-permute-start.3 = (bf16[2,8,48,128]{3,2,1,0:T(8,128)(2,1)S(1)}, bf16[2,8,48,128]{3,2,1,0:T(8,128)(2,1)S(1)}, u32[]{:S(2)}, u32[]{:S(2)}) collective-permute-start(bf16[2,8,48,128]{3,2,1,0:T(8,128)(2,1)S(1)} %fusion.32), channel_id=1, source_target_pairs={{0,16},{16,32},{32,48},{48,64},{64,80},{80,96},{96,112},{112,128},... | collective-permute-start | bytes 589832 | tf_op jit(solution)/shard_map/ppermute | solution.py:12
  434.4 7.7 %collective-permute-start.4 = (bf16[4,1,48,128]{3,2,1,0:T(8,128)(2,1)S(1)}, bf16[4,1,48,128]{3,2,1,0:T(8,128)(2,1)S(1)}, u32[]{:S(2)}, u32[]{:S(2)}) collective-permute-start(bf16[4,1,48,128]{3,2,1,0:T(8,128)(2,1)S(1)} %get-tuple-element.56), channel_id=1, source_target_pairs={{0,1},{1,2},{2,3},{3,4},{4,5},{5,6},{6,7},{7,8},{8,9},{9,10},{10,1... | collective-permute-start | bytes 147464 | tf_op jit(solution)/shard_map/ppermute | solution.py:23
  439.3 6.6 %collective-permute-start.5 = (bf16[4,1,48,128]{3,2,1,0:T(8,128)(2,1)S(1)}, bf16[4,1,48,128]{3,2,1,0:T(8,128)(2,1)S(1)}, u32[]{:S(2)}, u32[]{:S(2)}) collective-permute-start(bf16[4,1,48,128]{3,2,1,0:T(8,128)(2,1)S(1)} %get-tuple-element.57), channel_id=1, source_target_pairs={{1,0},{2,1},{3,2},{4,3},{5,4},{6,5},{7,6},{8,7},{9,8},{10,9},{11,1... | collective-permute-start | bytes 147464 | tf_op jit(solution)/shard_map/ppermute | solution.py:25
  448.1 1.4 copy-start.20
  451.2 0.7 copy-start.18
  452.0 0.9 copy-start.16
  452.0 1.2 copy-start.15
  452.2 1.4 copy-start.14
  455.2 0.9 copy-start
  455.2 0.9 copy-start.21
